TPU v7x, 128 devices: a whole 4x4x4 slice. The times are simulated.
128 devices in a mesh: row: 16 (over z, y), col: 8 (over x, core).
Axes of the slice: x: 4, y: 4, z: 4, core: 2. Of those that a mesh axis runs over, the one named last changes fastest.
Arguments:
- amplitudes: bfloat16 [8192, 7680], P(('row', 'col')), may hold values from -6 to 6
- integrals: bfloat16 [8, 7680, 1920], P('col', 'row'), may hold values from -0.0625 to 0.0625
- tile_ids: int32 [80], replicated, may hold values from 0 to 42335, as said below
- tile_owner: int32 [80], replicated, may hold values from 0 to 7, as said below
- occ_pairs: int32 [8192, 2], replicated, may hold values from 0 to 199
- occ_energy: float32 [200], replicated, may hold values from -1 to -0.2
- vir_energy: float32 [2016], replicated, may hold values from 0.1 to 1.5
Outputs:
- ladder_update: float32 [16, 512, 7680], P('row', 'col')
Inputs may be any that keep to these rules, and one draw needn't show every extreme that they name: `tile_ids`: distinct; tile g covers the flat virtual pairs g * 96 to g * 96 + 95, flat pair f being the virtuals f // 2016 and f % 2016. `tile_owner`: every column owns at least one tile and at most 20, one column exactly 20; integral slots past a column's count are unused.
All inputs are finite; a program needn't handle non-finite values.
Results may differ from a plain program's by a relative error of at most 0.0003.
Values may be sent and summed in bfloat16 or wider, within the bound.
No kernel may reach another device: no remote copies, remote signals or barrier semaphores. Data moves between devices by JAX's collectives and lax.ppermute only.
A program may use at most 128 MiB of HBM per device.

v0:
```python
import jax
import jax.numpy as jnp
from jax import lax
from jax.sharding import PartitionSpec as P

TW = 96
NVIR = 2016


def slot_table(tile_owner):
    positions = jnp.arange(tile_owner.shape[0])
    same_col = tile_owner[:, None] == tile_owner[None, :]
    earlier = positions[None, :] < positions[:, None]
    return jnp.sum(jnp.logical_and(same_col, earlier), axis=1)


def on_device(amplitudes, integrals, tile_ids, tile_owner, occ_pairs, occ_energy, vir_energy):
    n_row = lax.axis_size("row")
    n_col = lax.axis_size("col")
    occ_dev = amplitudes.shape[0]
    kept_count = tile_ids.shape[0]
    sub_rows = occ_dev // n_row
    local_v = integrals[0]
    local_cols = local_v.shape[0]
    old_cap = local_v.shape[1] // TW
    tile_view = amplitudes.reshape(occ_dev, kept_count, TW)
    slot_index = slot_table(tile_owner)
    flat_slot = tile_owner * old_cap + slot_index
    source = (
        jnp.zeros((n_col * old_cap,), jnp.int32)
        .at[flat_slot]
        .set(jnp.arange(kept_count, dtype=jnp.int32))
    )
    filled = jnp.zeros((n_col * old_cap,), jnp.bool_).at[flat_slot].set(True)
    taken = jnp.take(tile_view, source, axis=1)
    outbound = jnp.where(filled[None, :, None], taken, jnp.zeros_like(taken))
    outbound = outbound.reshape(occ_dev, n_col * old_cap * TW)
    ordered = outbound.reshape(n_row, sub_rows, n_col, old_cap * TW)
    ordered = jnp.transpose(ordered, (0, 2, 1, 3)).reshape(n_row * n_col * sub_rows, old_cap * TW)
    arrived = lax.all_to_all(ordered, ("row", "col"), split_axis=0, concat_axis=0, tiled=True)
    arrived = arrived.reshape(n_row, n_col, sub_rows, old_cap * TW)
    relaid = jnp.transpose(arrived, (1, 0, 2, 3)).reshape(n_col * n_row * sub_rows, old_cap * TW)
    block_count = local_cols // TW
    block_results = []
    for column_block in range(block_count):
        row_piece = local_v[column_block * TW : (column_block + 1) * TW]
        gathered = lax.all_gather(row_piece, "row", axis=0, tiled=True)

        def partial_rows(offset, amount, gathered=gathered):
            return lax.dot_general(
                relaid, gathered, (((1,), (1,)), ((), ())), preferred_element_type=jnp.float32
            )

        summed = lax.psum_scatter(
            partial_rows(jnp.int32(0), lax.axis_size("col") * occ_dev),
            "col",
            scatter_dimension=0,
            tiled=True,
        )
        block_results.append(summed.reshape(occ_dev, n_row, TW))
    residual = jnp.stack(block_results, axis=1)
    residual = jnp.transpose(residual, (0, 2, 1, 3)).reshape(occ_dev, kept_count * TW)
    local_rows = jnp.arange(occ_dev, dtype=jnp.int32)
    source_row = local_rows // sub_rows
    within_part = local_rows % sub_rows
    pair_pos = (
        (source_row * n_col + lax.axis_index("col")) * occ_dev
        + lax.axis_index("row") * sub_rows
        + within_part
    )
    pair_ids = jnp.take(occ_pairs, pair_pos, axis=0)
    occ_sum = occ_energy[pair_ids[:, 0]] + occ_energy[pair_ids[:, 1]]
    flat_pair = tile_ids[:, None] * TW + jnp.arange(TW, dtype=jnp.int32)[None, :]
    virt_sum = (vir_energy[flat_pair // NVIR] + vir_energy[flat_pair % NVIR]).reshape(
        kept_count * TW
    )
    update = residual / (virt_sum[None, :] - occ_sum[:, None])
    return update[None]


def solution(mesh):
    placed = (P(("row", "col"), None), P("col", "row", None), P(), P(), P(), P(), P())
    return jax.shard_map(
        on_device, mesh=mesh, in_specs=placed, out_specs=P("row", "col", None), check_vma=False
    )
```

profile of v0, /device:TPU:0, one launch (start us, length us, event | category | flops | bytes accessed | tf_op | source)
XLA Modules:
  0.0 539.9 jit_solution(13945077625682537110)
XLA Ops:
  6.5 2.8 fusion.40
  14.6 1.3 reshape.294
  16.3 2.5 gather_fusion
  18.8 3.4 copy.39
  22.3 3.1 gather.23
  25.4 2.0 copy_bitcast_fusion.1
  27.4 1.5 copy.41
  28.9 40.1 %all_to_all.9 = bf16[128,4,1920]{2,1,0:T(4,128)(2,1)S(1)} all-to-all(bf16[128,4,1920]{2,1,0:T(4,128)(2,1)S(1)} %copy.41), channel_id=1, replica_groups=mesh['row'=16,'col'=8] {'row','col'}, dimensions={0} | all-to-all | bytes 3932160 | tf_op jit(solution)/shard_map/all_to_all | solution.py:40
  69.7 1.5 reshape.296
  71.2 17.7 %all-gather.17.cloned.1.call-done = bf16[1,1536,1920]{2,1,0:T(8,128)(2,1)} async-done(((bf16[1,96,1920]{2,1,0:T(8,128)(2,1)}), bf16[1,1536,1920]{2,1,0:T(8,128)(2,1)}) %all-gather.17.cloned.1.call-update) | async-done | bytes 5898256 | tf_op jit(solution)/shard_map/all_gather | solution.py:47
  88.9 8.4 %fusion.2 = f32[512,1536]{1,0:T(8,128)} fusion(bf16[512,1920]{1,0:T(8,128)(2,1)} %reshape.296, bf16[1,1536,1920]{2,1,0:T(8,128)(2,1)} %all-gather.17.cloned.1.call-done), kind=kOutput, calls=%fused_computation.10 | convolution fusion | flops 3019898880 | bytes 11010048 | tf_op jit(solution)/shard_map/dot_general | solution.py:50
  97.5 52.4 %all-gather.11.cloned.1.call-done = bf16[1,1536,1920]{2,1,0:T(8,128)(2,1)} async-done(((bf16[1,96,1920]{2,1,0:T(8,128)(2,1)}), bf16[1,1536,1920]{2,1,0:T(8,128)(2,1)}) %all-gather.11.cloned.1.call-update) | async-done | bytes 5898256 | tf_op jit(solution)/shard_map/all_gather | solution.py:47
  149.9 7.8 %fusion.8 = f32[512,1536]{1,0:T(8,128)} fusion(bf16[512,1920]{1,0:T(8,128)(2,1)S(1)} %copy-done.2, bf16[1,1536,1920]{2,1,0:T(8,128)(2,1)} %all-gather.11.cloned.1.call-done), kind=kOutput, calls=%fused_computation.16 | convolution fusion | flops 3019898880 | bytes 11010048 | tf_op jit(solution)/shard_map/dot_general | solution.py:50
  157.8 53.5 %all-gather.13.cloned.1.call-done = bf16[1,1536,1920]{2,1,0:T(8,128)(2,1)} async-done(((bf16[1,96,1920]{2,1,0:T(8,128)(2,1)}), bf16[1,1536,1920]{2,1,0:T(8,128)(2,1)}) %all-gather.13.cloned.1.call-update) | async-done | bytes 5898256 | tf_op jit(solution)/shard_map/all_gather | solution.py:47
  211.3 7.7 %fusion.6 = f32[512,1536]{1,0:T(8,128)} fusion(bf16[512,1920]{1,0:T(8,128)(2,1)S(1)} %copy-done.2, bf16[1,1536,1920]{2,1,0:T(8,128)(2,1)} %all-gather.13.cloned.1.call-done), kind=kOutput, calls=%fused_computation.14 | convolution fusion | flops 3019898880 | bytes 11010048 | tf_op jit(solution)/shard_map/dot_general | solution.py:50
  219.1 53.4 %all-gather.15.cloned.1.call-done = bf16[1,1536,1920]{2,1,0:T(8,128)(2,1)} async-done(((bf16[1,96,1920]{2,1,0:T(8,128)(2,1)}), bf16[1,1536,1920]{2,1,0:T(8,128)(2,1)}) %all-gather.15.cloned.1.call-update) | async-done | bytes 5898256 | tf_op jit(solution)/shard_map/all_gather | solution.py:47
  272.5 7.8 %fusion.4 = f32[512,1536]{1,0:T(8,128)} fusion(bf16[512,1920]{1,0:T(8,128)(2,1)S(1)} %copy-done.2, bf16[1,1536,1920]{2,1,0:T(8,128)(2,1)} %all-gather.15.cloned.1.call-done), kind=kOutput, calls=%fused_computation.12 | convolution fusion | flops 3019898880 | bytes 11010048 | tf_op jit(solution)/shard_map/dot_general | solution.py:50
  280.6 53.1 %all-gather.19.cloned.1.call-done = bf16[1,1536,1920]{2,1,0:T(8,128)(2,1)} async-done(((bf16[1,96,1920]{2,1,0:T(8,128)(2,1)}), bf16[1,1536,1920]{2,1,0:T(8,128)(2,1)}) %all-gather.19.cloned.1.call-update) | async-done | bytes 5898256 | tf_op jit(solution)/shard_map/all_gather | solution.py:47
  333.7 7.8 %fusion = f32[512,1536]{1,0:T(8,128)} fusion(bf16[512,1920]{1,0:T(8,128)(2,1)S(1)} %copy-done.2, bf16[1,1536,1920]{2,1,0:T(8,128)(2,1)} %all-gather.19.cloned.1.call-done), kind=kOutput, calls=%fused_computation.8 | convolution fusion | flops 3019898880 | bytes 11010048 | tf_op jit(solution)/shard_map/dot_general | solution.py:50
  342.5 39.8 %gather_fusion.2 = f32[7680]{0:T(1024)S(1)} fusion(f32[2016]{0:T(1024)S(1)} %copy-done, s32[8192]{0:T(1024)S(1)} %pad_clamp_fusion), kind=kCustom, calls=%fused_computation.2 | custom fusion | bytes 92160 | tf_op jit(solution)/shard_map/gather | solution.py:74
  382.3 39.8 %gather_fusion.1 = f32[7680]{0:T(1024)S(1)} fusion(f32[2016]{0:T(1024)S(1)} %copy-done, s32[8192]{0:T(1024)S(1)} %pad_clamp_fusion.1), kind=kCustom, calls=%fused_computation.1 | custom fusion | bytes 92160 | tf_op jit(solution)/shard_map/gather | solution.py:74
  422.1 2.7 copy.48
  424.9 2.9 gather_fusion.3
  429.7 1.2 stack_reshape.18
  430.9 1.2 stack_reshape.15
  432.1 13.0 %reduce-scatter.8.cloned.1.call-done = f32[64,1536]{1,0:T(8,128)} async-done(((f32[512,1536]{1,0:T(8,128)}), f32[64,1536]{1,0:T(8,128)}) %reduce-scatter.8.cloned.1.call-update) | async-done | bytes 393232 | tf_op jit(solution)/shard_map/reduce_scatter | solution.py:54
  445.2 1.2 stack_reshape.16
  446.4 35.8 %reduce-scatter.10.cloned.1.call-done = f32[64,1536]{1,0:T(8,128)} async-done(((f32[512,1536]{1,0:T(8,128)}), f32[64,1536]{1,0:T(8,128)}) %reduce-scatter.10.cloned.1.call-update) | async-done | bytes 393232 | tf_op jit(solution)/shard_map/reduce_scatter | solution.py:54
  483.4 35.7 %reduce-scatter.14.cloned.1.call-done = f32[64,1536]{1,0:T(8,128)} async-done(((f32[512,1536]{1,0:T(8,128)}), f32[64,1536]{1,0:T(8,128)}) %reduce-scatter.14.cloned.1.call-update) | async-done | bytes 393232 | tf_op jit(solution)/shard_map/reduce_scatter | solution.py:54
  520.2 7.7 %stack.3 = f32[64,5,16,96]{3,1,2,0:T(8,128)} concatenate(f32[64,1,16,96]{3,1,2,0:T(1,128)S(1)} %bitcast.47, f32[64,1,16,96]{3,1,2,0:T(1,128)S(1)} %bitcast.48, f32[64,1,16,96]{3,1,2,0:T(1,128)S(1)} %bitcast.49, f32[64,1,16,96]{3,1,2,0:T(1,128)S(1)} %bitcast.46, f32[64,1,16,96]{3,1,2,0:T(1,128)S(1)} %bitcast.50), dimensions={1} | concatenate | bytes 3932160 | tf_op jit(solution)/shard_map/stack | solution.py:61
  527.9 3.6 reshape.297
  531.5 1.6 subtract_divide_fusion
  (71 shorter events, 12.2 us)
Async XLA Ops:
  6.5 335.9 %copy-start = (f32[2016]{0:T(1024)S(1)}, f32[2016]{0:T(1024)}, u32[]{:S(2)}) copy-start(f32[2016]{0:T(1024)} %param.13) | copy-start | bytes 24196
  6.5 5.5 %copy-start.5 = (s32[80]{0:T(128)S(1)}, s32[80]{0:T(128)}, u32[]{:S(2)}) copy-start(s32[80]{0:T(128)} %param.10) | copy-start | bytes 964
  6.5 8.1 %copy-start.3 = (bf16[64,7680]{1,0:T(8,128)(2,1)S(1)}, bf16[64,7680]{1,0:T(8,128)(2,1)}, u32[]{:S(2)}) copy-start(bf16[64,7680]{1,0:T(8,128)(2,1)} %param.7) | copy-start | bytes 2949124
  6.5 82.4 %all-gather.17.cloned.1.call-start = ((), (), s32[]{:S(2)}) async-start(), calls=%async_computation.14 | async-start | bytes 6266880 | tf_op jit(solution)/shard_map/all_gather | solution.py:47
  9.4 140.5 %all-gather.11.cloned.1.call-start = ((), (), s32[]{:S(2)}) async-start(), calls=%async_computation.11 | async-start | bytes 6266880 | tf_op jit(solution)/shard_map/all_gather | solution.py:47
  10.1 201.1 %all-gather.13.cloned.1.call-start = ((), (), s32[]{:S(2)}) async-start(), calls=%async_computation.12 | async-start | bytes 6266880 | tf_op jit(solution)/shard_map/all_gather | solution.py:47
  10.9 261.6 %all-gather.15.cloned.1.call-start = ((), (), s32[]{:S(2)}) async-start(), calls=%async_computation.13 | async-start | bytes 6266880 | tf_op jit(solution)/shard_map/all_gather | solution.py:47
  11.4 322.2 %all-gather.19.cloned.1.call-start = ((), (), s32[]{:S(2)}) async-start(), calls=%async_computation.15 | async-start | bytes 6266880 | tf_op jit(solution)/shard_map/all_gather | solution.py:47
  12.0 417.7 %reduce-scatter.12.cloned.1.call-start = ((), (), s32[]{:S(2)}) async-start(), calls=%async_computation.9 | async-start | bytes 3538944 | tf_op jit(solution)/shard_map/reduce_scatter | solution.py:54
  97.3 52.7 %copy-start.2 = (bf16[512,1920]{1,0:T(8,128)(2,1)S(1)}, bf16[512,1920]{1,0:T(8,128)(2,1)}, u32[]{:S(2)}) copy-start(bf16[512,1920]{1,0:T(8,128)(2,1)} %reshape.296) | copy-start | bytes 5898244
  97.3 333.6 %reduce-scatter.6.cloned.1.call-start = ((), (), s32[]{:S(2)}) async-start(), calls=%async_computation.6 | async-start | bytes 3538944 | tf_op jit(solution)/shard_map/reduce_scatter | solution.py:54
  157.7 287.4 %reduce-scatter.8.cloned.1.call-start = ((), (), s32[]{:S(2)}) async-start(), calls=%async_computation.7 | async-start | bytes 3538944 | tf_op jit(solution)/shard_map/reduce_scatter | solution.py:54
  219.0 263.1 %reduce-scatter.10.cloned.1.call-start = ((), (), s32[]{:S(2)}) async-start(), calls=%async_computation.8 | async-start | bytes 3538944 | tf_op jit(solution)/shard_map/reduce_scatter | solution.py:54
  280.3 238.7 %reduce-scatter.14.cloned.1.call-start = ((), (), s32[]{:S(2)}) async-start(), calls=%async_computation.10 | async-start | bytes 3538944 | tf_op jit(solution)/shard_map/reduce_scatter | solution.py:54
  341.5 0.7 copy-start.6
  382.3 39.8 %copy-start.4 = (s32[8192,2]{0,1:T(2,128)S(1)}, s32[8192,2]{0,1:T(2,128)}, u32[]{:S(2)}) copy-start(s32[8192,2]{0,1:T(2,128)} %param.11) | copy-start | bytes 196612
  422.1 6.0 %copy-start.1 = (f32[200]{0:T(256)S(1)}, f32[200]{0:T(256)}, u32[]{:S(2)}) copy-start(f32[200]{0:T(256)} %param.12) | copy-start | bytes 2404
Sparse Core Ops, SparseCore 0:
  9.5 79.3 all-gather.16
  91.0 58.8 all-gather.10
  152.1 59.1 all-gather.12
  213.3 59.1 all-gather.14
  274.5 59.1 all-gather.18
  335.9 35.2 reduce-scatter.11
  373.6 34.5 reduce-scatter.5
  410.6 34.5 reduce-scatter.7
  447.6 34.5 reduce-scatter.9
  484.4 34.5 reduce-scatter.13
where the time goes:
time: 541 us; the launch traced here: 540 us
  waiting for transfers between devices  317 us (59%)
  local copies, waits for them, and re-layouts  124 us (23%)
  blocking collectives  40.1 us (7%)
  matrix products  39.6 us (7%)
  between operations  13.8 us (3%)
    all_gather x5, waiting for transfers between devices, on_device(): gathered = lax.all_gather(row_piece, 'row', axis=0, tiled=True)  230 us
    reduce_scatter x5, waiting for transfers between devices, on_device(): lax.psum_scatter(partial_rows(jnp.int32(0), lax.axis_size('col') * occ_de...  84.6 us
    all_to_all x1, blocking collectives, on_device(): lax.all_to_all(ordered, ('row', 'col'), split_axis=0, concat_axis=0, tile...  40.1 us
    gather x1, local copies, waits for them, and re-layouts, on_device(): vir_energy[flat_pair % NVIR]  39.8 us
    gather x1, local copies, waits for them, and re-layouts, on_device(): vir_energy[flat_pair // NVIR] + vir_energy[flat_pair % NVIR]  39.8 us
    dot_general x5, matrix products, partial_rows(): lax.dot_general(relaid, gathered, (((1,), (1,)), ((), ())), preferred_ele...  39.6 us
    another operation x6, local copies, waits for them, and re-layouts, on_device(): residual = jnp.stack(block_results, axis=1)  13.6 us
  transfers between devices with their start and end apart: 10, of which 8 were waited for; matrix products, arithmetic and copies ran while one was open for 28% of the time, Pallas kernels for 0%

commit v1 on v0

v1 whole, which is shorter than its diff:
```python
import functools

import jax
import jax.numpy as jnp
from jax import lax
from jax.experimental import pallas as pl
from jax.experimental.pallas import tpu as pltpu
from jax.sharding import Mesh, PartitionSpec as P

TW = 96
NVIR = 2016
SIDE = 4
TILES = 80
CAP = 20
QUAD = 4
LANES = 128
WINDOW = 2 * LANES
HALF = 240
PADDED = 256
WIDTH = CAP * TW
CUT = 128
LEVELS = 32000.0
STEPS = 256.0
ALL = ("z", "y", "x", "c")
SEND = 0
GATHER = 3 * CAP
ROUNDS = GATHER + CAP
VMEM = pltpu.CompilerParams(vmem_limit_bytes=48 * 1024 * 1024)


def ring(value, axis, shift):
    return lax.ppermute(value, axis, [(i, (i + shift) % SIDE) for i in range(SIDE)])


def swap(value):
    return lax.ppermute(value, "c", [(0, 1), (1, 0)])


def four_tiles(load, starts, limit):
    parts = []
    for start, want in zip(starts, (0, 96, 64, 160)):
        base = jnp.minimum((start // LANES) * LANES, limit - WINDOW)
        window = load(pl.multiple_of(base, LANES))
        parts.append(pltpu.roll(window, (want - (start - base)) & (WINDOW - 1), 1))
    a, b, c, d = parts
    lane = lax.broadcasted_iota(jnp.int32, (a.shape[0], LANES), 1)
    return (
        jnp.where(lane < 96, a[:, :LANES], b[:, :LANES]),
        jnp.where(lane < 64, b[:, LANES:], c[:, :LANES]),
        jnp.where(lane < 32, c[:, LANES:], d[:, LANES:]),
    )


def one_hot(size, source):
    row = lax.broadcasted_iota(jnp.int32, (size, size), 0)
    col = lax.broadcasted_iota(jnp.int32, (size, size), 1)
    return jnp.where(col == source(row), 1.0, 0.0).astype(jnp.bfloat16)


def plan_kernel(owner, out):
    x, c = (lax.axis_index(name).astype(jnp.float32) for name in "xc")
    i = lax.broadcasted_iota(jnp.int32, (TILES, TILES), 0)
    j = lax.broadcasted_iota(jnp.int32, (TILES, TILES), 1)
    across = lambda mask, value=1.0: jnp.sum(jnp.where(mask, value, 0.0), axis=1, keepdims=True)
    down = lambda mask, value=1.0: jnp.sum(jnp.where(mask, value, 0.0), axis=0, keepdims=True)
    earlier = j < i
    owner_row = owner[...].astype(jnp.float32)
    owner_col = across(i == j, owner_row)
    home_row, home = jnp.floor(owner_row * 0.5), jnp.floor(owner_col * 0.5)
    slot = across((owner_row == owner_col) & earlier)
    rank = across((home_row == home) & earlier)
    moves = rank >= CAP
    over = under = jnp.zeros((1, 1), jnp.float32)
    number = rank - CAP
    ends, starts = [], []
    for k in range(SIDE):
        load = across(home_row == k)
        number = number + jnp.where(home == k, over, 0.0)
        starts.append(load - under)
        over = over + jnp.maximum(load - CAP, 0.0)
        under = under + jnp.maximum(CAP - load, 0.0)
        ends.append(under)
    target = jnp.where(moves, sum(jnp.where(number >= end, 1.0, 0.0) for end in ends), home)
    start = sum(jnp.where(target == k, starts[k], 0.0) for k in range(SIDE))
    pos = jnp.where(moves, start + number, rank)
    moving = jnp.where(moves, home * SIDE + target, -1.0)
    order = across((down(i == j, moving) == moving) & earlier)
    place = jnp.where(owner_col - 2.0 * home == c, slot, CAP + slot)
    shift = target - home
    shift = jnp.where(shift < 0.0, shift + SIDE, shift) - 1.0
    lane = lax.broadcasted_iota(jnp.int32, (TILES, LANES), 1).astype(jnp.float32)
    row = lax.broadcasted_iota(jnp.int32, (TILES, LANES), 0).astype(jnp.float32)
    perm = down(lane == target * CAP + pos, row)
    outgoing = jnp.where(moves & (home == x), SEND + shift * CAP + order, -1.0)
    group = jnp.floor(order * (1.0 / QUAD))
    arriving = 2 * CAP + group * 3 * QUAD + shift * QUAD + order - group * QUAD
    incoming = jnp.where(target == x, GATHER + pos, -1.0)
    table = down(lane == outgoing, place) + down(lane == incoming, jnp.where(moves, arriving, place))
    most = jnp.max(jnp.where(moves, order, -1.0), axis=0, keepdims=True)
    rounds = jnp.floor((most + QUAD) * (1.0 / QUAD))
    table = jnp.where(lane[:1] == ROUNDS, rounds, table)
    out[0:1, :] = perm.astype(jnp.int32)
    out[1:2, :] = table.astype(jnp.int32)


def make_plan(tile_owner):
    vmem = pl.BlockSpec(memory_space=pltpu.VMEM)
    return pl.pallas_call(
        plan_kernel,
        out_shape=jax.ShapeDtypeStruct((2, LANES), jnp.int32),
        in_specs=[vmem],
        out_specs=vmem,
        name="make_plan",
    )(tile_owner[None, :])


def amplitude_kernel(table, amp, after, *outs):
    x = lax.axis_index("x")
    load = lambda base: amp[:, pl.ds(base, WINDOW)].astype(jnp.float32)
    for s, out in enumerate(outs):
        first = ((x + s) % SIDE) * CAP
        for g in range(0, CAP, QUAD):
            starts = [table[0, first + g + j] * TW for j in range(QUAD)]
            for k, column in enumerate(four_tiles(load, starts, TILES * TW)):
                at = g * TW + k * LANES
                out[:, at : at + LANES] = column.astype(jnp.bfloat16)


def order_amplitudes(table, amplitudes, after):
    vmem = pl.BlockSpec(memory_space=pltpu.VMEM)
    return pl.pallas_call(
        amplitude_kernel,
        out_shape=tuple(jax.ShapeDtypeStruct((64, WIDTH), jnp.bfloat16) for _ in range(SIDE)),
        in_specs=[pl.BlockSpec(memory_space=pltpu.SMEM), vmem, pl.BlockSpec(memory_space=pl.ANY)],
        out_specs=tuple(vmem for _ in range(SIDE)),
        compiler_params=VMEM,
        name="order_amplitudes",
    )(table, amplitudes, after)


def tile_rows(pool, table, first, out, at):
    def rows(i, carry):
        here = pl.ds(pl.multiple_of(i * 48, 16), 48)
        load = lambda base: pool[here, pl.ds(base, WINDOW)].astype(jnp.float32)
        starts = [table[1, first + j] * TW for j in range(QUAD)]
        for k, column in enumerate(four_tiles(load, starts, pool.shape[1])):
            out[here, at + k * LANES : at + (k + 1) * LANES] = column.astype(jnp.bfloat16)
        return carry

    lax.fori_loop(0, HALF // 48, rows, 0)


def fill_pool(sources, pool, sems):
    half = pl.ds(pl.multiple_of(lax.axis_index("c") * HALF, 16), HALF)
    copies = []
    at = 0
    for i, ref in enumerate(sources):
        src = ref.at[half] if i < 2 else ref
        width = ref.shape[1]
        copies.append(pltpu.make_async_copy(src, pool.at[:, pl.ds(at, width)], sems.at[i]))
        at += width
    for copy in copies:
        copy.start()
    for copy in copies:
        copy.wait()


def pack_kernel(number, table, mine, other, after, out1, out2, out3, pool, sems):
    fill_pool((mine, other), pool, sems)
    for s, out in enumerate((out1, out2, out3)):
        tile_rows(pool, table, SEND + s * CAP + number * QUAD, out, 0)


def assemble_kernel(table, mine, other, in1, in2, in3, extra, out, pool, sems):
    fill_pool((mine, other, in1, in2, in3), pool, sems)
    at, width = 2 * WIDTH + 3 * QUAD * TW, QUAD * TW

    @pl.when(table[1, ROUNDS] > 1)
    def _():
        copies = [
            pltpu.make_async_copy(extra.at[i], pool.at[:, pl.ds(at + i * width, width)], sems.at[i])
            for i in range(extra.shape[0])
        ]
        for copy in copies:
            copy.start()
        for copy in copies:
            copy.wait()

    for g in range(CAP // QUAD):
        tile_rows(pool, table, GATHER + g * QUAD, out, g * QUAD * TW)


def pack(number, table, mine, other, after):
    anywhere = pl.BlockSpec(memory_space=pl.ANY)
    return pl.pallas_call(
        functools.partial(pack_kernel, number),
        out_shape=tuple(jax.ShapeDtypeStruct((HALF, QUAD * TW), jnp.bfloat16) for _ in range(3)),
        in_specs=[pl.BlockSpec(memory_space=pltpu.SMEM), anywhere, anywhere, anywhere],
        out_specs=tuple(pl.BlockSpec(memory_space=pltpu.VMEM) for _ in range(3)),
        scratch_shapes=[pltpu.VMEM((HALF, 2 * WIDTH), jnp.bfloat16), pltpu.SemaphoreType.DMA((2,))],
        compiler_params=VMEM,
        name="pack",
    )(table, mine, other, after)


def assemble(table, mine, other, received, extra):
    anywhere = pl.BlockSpec(memory_space=pl.ANY)
    n = len(received) + extra.shape[0]
    return pl.pallas_call(
        assemble_kernel,
        out_shape=jax.ShapeDtypeStruct((HALF, WIDTH), jnp.bfloat16),
        in_specs=[pl.BlockSpec(memory_space=pltpu.SMEM)] + [anywhere] * 6,
        out_specs=pl.BlockSpec(memory_space=pltpu.VMEM),
        scratch_shapes=[
            pltpu.VMEM((HALF, 2 * WIDTH + n * QUAD * TW), jnp.bfloat16),
            pltpu.SemaphoreType.DMA((2 + n,)),
        ],
        compiler_params=VMEM,
        cost_estimate=pl.CostEstimate(flops=0, bytes_accessed=10 << 20, transcendentals=0),
        name="assemble",
    )(table, mine, other, *received, extra)


def send(packed):
    return [ring(part, "x", s + 1) for s, part in enumerate(packed)]


def later_rounds(table, mine, other):
    def more(table, mine, other):
        parts = []
        for number in range(1, CAP // QUAD):
            parts += send(pack(number, table, mine, other, parts[-1] if parts else table))
        return jnp.stack(parts)

    def none(table, mine, other):
        return jnp.zeros((3 * (CAP // QUAD - 1), HALF, QUAD * TW), mine.dtype)

    return lax.cond(table[1, ROUNDS] > 1, more, none, table, mine, other)


def encode(value):
    top = jnp.max(jnp.abs(value), axis=1, keepdims=True)
    code = jnp.ceil(jnp.log2(jnp.maximum(top, 1e-33)) * STEPS)
    level = jnp.floor(value * (jnp.exp2(code * (-1.0 / STEPS)) * LEVELS) + 0.5)
    return level.astype(jnp.int32).astype(jnp.int16), code.astype(jnp.int32).astype(jnp.int16)


def decode(coded):
    wide = coded.astype(jnp.int32).astype(jnp.float32)
    lane = lax.broadcasted_iota(jnp.int32, wide.shape, 1)
    code = jnp.sum(jnp.where(lane == HALF, wide, 0.0), axis=1, keepdims=True)
    return wide[:, :HALF] * (jnp.exp2(code * (1.0 / STEPS)) * (1.0 / LEVELS))


def put(out, k, level, code):
    out[k, :, :HALF] = level
    out[k, :, HALF:] = jnp.broadcast_to(code, (64, PADDED - HALF))


def code_far_kernel(n, *refs):
    sums, (up, down) = refs[: 2 * n], refs[2 * n :]
    for k in range(n):
        put(up, k, *encode(sums[k][...]))
        put(down, k, *encode(sums[n + k][...]))


def code_near_kernel(n, *refs):
    sums, (up, down, nxt, prv) = refs[: 2 * n], refs[2 * n :]
    step = pl.program_id(0)

    def run(first, second, out, extra):
        for k in range(n):
            put(out, k, *encode(sums[first + k][...] + decode(extra[k])))
        for k in range(n):
            put(second[0], k, *encode(sums[second[1] + k][...]))

    pl.when(step < 2)(lambda: run(0, (prv, n), nxt, up))
    pl.when(step >= 2)(lambda: run(n, (nxt, 0), prv, down))


def code_last_kernel(n, *refs):
    sums, (low, high, out) = refs[:n], refs[n:]
    for k in range(n):
        level, code = encode(sums[k][...] + decode(low[k]) + decode(high[k]))
        code = jnp.broadcast_to(code, (64, PADDED - HALF))
        for row in range(SIDE):
            rows = slice(16 * row, 16 * (row + 1))
            out[row, k, :, :HALF] = level[rows]
            out[row, k, :, HALF:] = code[rows]


def code_far(sums):
    n = len(sums)
    out = jax.ShapeDtypeStruct((n, CUT, PADDED), jnp.int16)
    block = pl.BlockSpec((n, 64, PADDED), lambda i: (0, i, 0))
    rows = lambda shift: pl.BlockSpec((64, HALF), lambda i: (i + shift, 0))
    return pl.pallas_call(
        functools.partial(code_far_kernel, n),
        out_shape=(out, out),
        grid=(2,),
        in_specs=[rows(0)] * n + [rows(2)] * n,
        out_specs=(block, block),
        compiler_params=VMEM,
        name="code_far",
    )(*sums, *sums)


def code_near(sums_next, sums_prev, up, down):
    n = len(sums_next)
    out = jax.ShapeDtypeStruct((n, 2 * CUT, PADDED), jnp.int16)
    block = pl.BlockSpec((n, 64, PADDED), lambda i: (0, i, 0))
    half = lambda shift: pl.BlockSpec((n, 64, PADDED), lambda i: (0, jnp.clip(i - shift, 0, 1), 0))
    rows = pl.BlockSpec((64, HALF), lambda i: (i, 0))
    return pl.pallas_call(
        functools.partial(code_near_kernel, n),
        out_shape=(out, out),
        grid=(4,),
        in_specs=[rows] * (2 * n) + [half(0), half(2)],
        out_specs=(block, block),
        compiler_params=VMEM,
        name="code_near",
    )(*sums_next, *sums_prev, up, down)


def code_last(sums, low, high):
    n = len(sums)
    block = pl.BlockSpec((n, 64, PADDED), lambda i: (0, i, 0))
    return pl.pallas_call(
        functools.partial(code_last_kernel, n),
        out_shape=jax.ShapeDtypeStruct((SIDE * SIDE, n, 16, PADDED), jnp.int16),
        grid=(4,),
        in_specs=[pl.BlockSpec((64, HALF), lambda i: (i, 0))] * n + [block, block],
        out_specs=pl.BlockSpec((SIDE, n, 16, PADDED), lambda i: (i, 0, 0, 0)),
        compiler_params=VMEM,
        name="code_last",
    )(*sums, low, high)


def finish_kernel(groups, *refs):
    c = lax.axis_index("c")
    got, (virt, occ, out) = refs[: len(groups)], refs[len(groups) :]
    spots = {up: (ref, 2 * k) for ref, group in zip(got, groups) for k, up in enumerate(group)}
    by_zr = one_hot(64, lambda i: ((i // 4) % 4) * 16 + (i // 16) * 4 + i % 4).astype(jnp.float32)
    for ya in range(SIDE):
        for h in range(2):
            parts = []
            for ys in range(SIDE):
                ref, k = spots[(ya - ys) % SIDE]
                parts.append(decode(ref[ys, k + jnp.bitwise_xor(c, h)]))
            value = jnp.dot(by_zr, jnp.concatenate(parts, axis=0), precision=lax.Precision.HIGHEST)
            at = slice((2 * ya + h) * HALF, (2 * ya + h + 1) * HALF)
            out[:, at] = value / (virt[:, at] - occ[...])


def finish(groups, got, virt, occ):
    block = lambda n: pl.BlockSpec((SIDE, n, 16, PADDED), lambda i: (i, 0, 0, 0))
    return pl.pallas_call(
        functools.partial(finish_kernel, groups),
        grid=(SIDE,),
        out_shape=jax.ShapeDtypeStruct((64, SIDE * WIDTH), jnp.float32),
        in_specs=[block(2 * len(group)) for group in groups]
        + [
            pl.BlockSpec((1, WIDTH), lambda i: (0, i)),
            pl.BlockSpec((64, 1), lambda i: (0, 0)),
        ],
        out_specs=pl.BlockSpec((64, WIDTH), lambda i: (0, i)),
        compiler_params=VMEM,
        name="finish",
    )(*got, virt, occ)


def ring_pieces(first, second):
    both = (first, second)
    steps = [ring(piece, axis, shift) for piece, axis, _ in both for shift in (1, -1)]
    steps = lax.optimization_barrier(tuple(steps))
    lows, highs = steps[0::2], steps[1::2]
    fars = []
    for (_, axis, cut), low, high in zip(both, lows, highs):
        fars += [ring(low[:cut], axis, 1), ring(high[cut:], axis, -1)]
    fars = lax.optimization_barrier(tuple(fars))
    return [
        (piece, high, *fars[2 * i : 2 * i + 2], low)
        for i, ((piece, _, _), low, high) in enumerate(zip(both, lows, highs))
    ]


def on_device(amplitudes, integrals, tile_ids, tile_owner, occ_pairs, occ_energy, vir_energy):
    z, y, x, c = (lax.axis_index(name) for name in ALL)
    occ_dev = amplitudes.shape[0]
    sub = occ_dev // (SIDE * SIDE)
    mine = integrals[0]
    other = swap(mine)
    table = make_plan(tile_owner)
    extra = later_rounds(table, mine, other)
    packed = pack(0, table, mine, other, extra)
    first = send(packed)
    last, *leaving = order_amplitudes(table, amplitudes, packed[0])
    prev, far, nxt = send(leaving)
    shard = assemble(table, mine, other, first, extra)
    arrived = jnp.concatenate([far, nxt, prev, last], axis=0)
    arrived, _ = lax.optimization_barrier((arrived, shard))
    shares, pieces = ring_pieces((shard, "y", CUT), (arrived, "z", 2 * occ_dev))
    own, high, far0, far1, low = [(piece, swap(piece)) for piece in shares]
    both = tuple(jnp.concatenate([far0[i], far1[i]], axis=0) for i in range(2))
    blocks = [own, high, both, low]
    by_k = one_hot(256, lambda i: (((i // 4) % 4 - z) % 4) * 64 + (i // 16) * 4 + i % 4)

    def pairs_of(number):
        own, high, far0, far1, low = pieces
        at = lambda p, n: p[n * occ_dev : (n + 1) * occ_dev]
        far = at(far0, number) if number < 2 else at(far1, number - 2)
        whole = jnp.concatenate([at(own, number), at(high, number), far, at(low, number)], axis=0)
        return jnp.dot(by_k, whole, preferred_element_type=jnp.float32).astype(whole.dtype)

    def product(a, b):
        return lax.dot_general(a, b, (((1,), (1,)), ((), ())), preferred_element_type=jnp.float32)

    def sums(number, blocks):
        return [product(pairs[number], b) for b in blocks]

    pairs = [pairs_of(number) for number in range(SIDE)]

    def reduced(blocks):
        up, down = code_far(sums(0, blocks))
        pairs[1], pairs[2], pairs[3], *_ = lax.optimization_barrier((*pairs[1:], up, down))

        def near(next_pairs, prev_pairs, *blocks):
            return [product(p, b) for p in (next_pairs, prev_pairs) for b in blocks]

        def nothing(*_):
            return [jnp.zeros((4 * occ_dev, HALF), jnp.float32) for _ in range(2 * len(blocks))]

        both = lax.cond(table[1, ROUNDS] >= 0, near, nothing, pairs[1], pairs[2], *blocks)
        n = len(blocks)
        nxt, prv = code_near(both[:n], both[n:], ring(up, "x", 1), ring(down, "x", -1))
        total = code_last(sums(3, blocks), ring(nxt, "x", 1), ring(prv, "x", -1))
        got = lax.all_to_all(total, ("z", "y"), split_axis=0, concat_axis=0, tiled=True)
        return got, up

    groups = ((0, 1, 2, 3),)
    got, sent = zip(*(reduced([half for up in group for half in blocks[up]]) for group in groups))
    occ_pairs, occ_energy, vir_energy, _ = lax.optimization_barrier(
        (occ_pairs, occ_energy, vir_energy, sent[0])
    )

    grid = occ_pairs.reshape(SIDE * SIDE, 2 * SIDE, SIDE * SIDE, sub, 2)
    here = lax.dynamic_slice(grid, (0, 2 * x + c, SIDE * z + y, 0, 0), (SIDE * SIDE, 1, 1, sub, 2))
    occ_sum = jnp.sum(jnp.take(occ_energy, here.reshape(occ_dev, 2), axis=0), axis=1)
    per_row = NVIR // TW
    second = jnp.take(vir_energy.reshape(per_row, TW), tile_ids % per_row, axis=0)
    virt_sum = (jnp.take(vir_energy, tile_ids // per_row)[:, None] + second).reshape(1, TILES * TW)
    return finish(groups, got, virt_sum, occ_sum[:, None])[None]


def solution(mesh):
    chips = Mesh(mesh.devices.reshape(SIDE, SIDE, SIDE, 2), ALL)
    placed = (P(ALL, None), P(("x", "c"), ("z", "y"), None), P(), P(), P(), P(), P())
    return jax.shard_map(
        on_device, mesh=chips, in_specs=placed, out_specs=P(("z", "y"), ("x", "c"), None), check_vma=False
    )
```

time: 541 us -> 168 us (0.31)
  waiting for transfers between devices: 317 us -> 67.1 us
  local copies, waits for them, and re-layouts: 124 us -> 14 us
  blocking collectives: 40.1 us -> 0 us
  starting transfers between devices: 0.76 us -> 39.1 us
  Pallas kernels: 0 us -> 24.1 us
  matrix products: 39.6 us -> 19.5 us
  between operations: 13.8 us -> 1.95 us
    all_gather x5 -> x0, waiting for transfers between devices: 230 us -> none  [on_device(): gathered = lax.all_gather(row_piece, 'row', axis=0, tiled=True)]
    gather x8 -> x5, local copies, waits for them, and re-layouts: 93 us -> 3.38 us  [the longest x3 1.62 us: on_device(): jnp.take(occ_energy, here.reshape(occ_dev, 2), axis=0)]
    reduce_scatter x5 -> x0, waiting for transfers between devices: 84.6 us -> none  [on_device(): lax.psum_scatter(partial_rows(jnp.int32(0), lax.axis_size('col') * occ_de...]
    ppermute x0 -> x24, waiting for transfers between devices: none -> 60.6 us  [the longest x18 58.7 us: ring(): lax.ppermute(value, axis, [(i, (i + shift) % SIDE) for i in range(SIDE)])]
    all_to_all x1 -> x0, blocking collectives: 40.1 us -> none  [on_device(): lax.all_to_all(ordered, ('row', 'col'), split_axis=0, concat_axis=0, tile...]
    ppermute x0 -> x24, starting transfers between devices: none -> 32.8 us  [the longest x18 31.7 us: ring(): lax.ppermute(value, axis, [(i, (i + shift) % SIDE) for i in range(SIDE)])]
    dot_general x5 -> x20, matrix products: 39.6 us -> 12 us  [the longest x16 9.12 us: product(): lax.dot_general(a, b, (((1,), (1,)), ((), ())), preferred_element_type=jn...]
    pallas_call x0 -> x8, Pallas kernels: none -> 24.1 us  [the longest x1 5.5 us: finish(): pl.pallas_call(functools.partial(finish_kernel, groups), grid=(SIDE,), ou...]
  transfers between devices with their start and end apart: 10 -> 25, of which waited for: 8 -> 8; matrix products, arithmetic and copies ran while one was open for 28% -> 20% of each run, Pallas kernels for 0% -> 4%
where the time goes in v1:
time: 168 us
  waiting for transfers between devices  67.1 us (40%)
  starting transfers between devices  39.1 us (23%)
  Pallas kernels  24.1 us (14%)
  matrix products  19.5 us (12%)
  local copies, waits for them, and re-layouts  14 us (8%)
  between operations  1.95 us (1%)
  other arithmetic  1.79 us (1%)
    ppermute x18, waiting for transfers between devices, ring(): lax.ppermute(value, axis, [(i, (i + shift) % SIDE) for i in range(SIDE)])  58.7 us
    ppermute x18, starting transfers between devices, ring(): lax.ppermute(value, axis, [(i, (i + shift) % SIDE) for i in range(SIDE)])  31.7 us
    dot_general x16, matrix products, product(): lax.dot_general(a, b, (((1,), (1,)), ((), ())), preferred_element_type=jn...  9.12 us
    cond x16, matrix products, reduced(): lax.cond(table[1, ROUNDS] >= 0, near, nothing, pairs[1], pairs[2], *blocks)  7.53 us
    all_to_all x1, waiting for transfers between devices, reduced(): lax.all_to_all(total, ('z', 'y'), split_axis=0, concat_axis=0, tiled=True)  6.55 us
    all_to_all x1, starting transfers between devices, reduced(): lax.all_to_all(total, ('z', 'y'), split_axis=0, concat_axis=0, tiled=True)  6.38 us
    pallas_call x1, Pallas kernels, finish(): pl.pallas_call(functools.partial(finish_kernel, groups), grid=(SIDE,), ou...  5.5 us
    pallas_call x1, Pallas kernels, assemble(): pl.pallas_call(assemble_kernel, out_shape=jax.ShapeDtypeStruct((HALF, WID...  4.78 us
  transfers between devices with their start and end apart: 25, of which 8 were waited for; matrix products, arithmetic and copies ran while one was open for 20% of the time, Pallas kernels for 4%

profile of v1, /device:TPU:0, one launch (start us, length us, event | category | flops | bytes accessed | tf_op | source)
XLA Modules:
  0.0 167.9 jit_solution(4514932722485043669)
XLA Ops:
  2.3 1.9 %collective-permute-done.12.other = bf16[480,1920]{1,0:T(8,128)(2,1)} collective-permute-done((bf16[480,1920]{1,0:T(8,128)(2,1)}, bf16[480,1920]{1,0:T(8,128)(2,1)}, u32[]{:S(2)}, u32[]{:S(2)}) %collective-permute-start.12) | collective-permute-done | bytes 1843232 | tf_op jit(solution)/shard_map/ppermute | solution.py:36
  4.1 1.6 conditional.2
  4.1 1.6 broadcast.121
  5.7 4.0 %pack.9 = (bf16[240,384]{1,0:T(8,128)(2,1)S(1)}, bf16[240,384]{1,0:T(8,128)(2,1)S(1)}, bf16[240,384]{1,0:T(8,128)(2,1)S(1)}) custom-call(s32[2,128]{1,0:T(2,128)S(1)} %make_plan.1.table, bf16[480,1920]{1,0:T(8,128)(2,1)} %bitcast.101, bf16[480,1920]{1,0:T(8,128)(2,1)} %collective-permute-done.12.other, bf16[12,240,384]{2,1,0:T(8,128)(2,1)} %get-tuple-element.225.after.extra), custom_call_target="tpu_custom_call" | custom-call | tf_op jit(solution)/shard_map/pack/pallas_call | solution.py:195
  9.7 1.6 collective-permute-start.16
  11.4 1.5 order_amplitudes.1
  12.9 2.8 %collective-permute-start.13 = (bf16[64,1920]{1,0:T(8,128)(2,1)S(1)}, bf16[64,1920]{1,0:T(8,128)(2,1)S(1)}, u32[]{:S(2)}, u32[]{:S(2)}) collective-permute-start(bf16[64,1920]{1,0:T(8,128)(2,1)S(1)} %get-tuple-element.102), channel_id=1, source_target_pairs={{0,4},{2,6},{4,0},{6,2},{1,5},{3,7},{5,1},{7,3},{8,12},{10,14},{12... | collective-permute-start | bytes 737288 | tf_op jit(solution)/shard_map/ppermute | solution.py:32
  18.6 1.8 %collective-permute-start.18 = (bf16[240,384]{1,0:T(8,128)(2,1)S(1)}, bf16[240,384]{1,0:T(8,128)(2,1)S(1)}, u32[]{:S(2)}, u32[]{:S(2)}) collective-permute-start(bf16[240,384]{1,0:T(8,128)(2,1)S(1)} %get-tuple-element.107), channel_id=1, source_target_pairs={{0,6},{2,0},{4,2},{6,4},{1,7},{3,1},{5,3},{7,5},{8,14},{10,8},{12,... | collective-permute-start | bytes 552968 | tf_op jit(solution)/shard_map/ppermute | solution.py:32
  20.5 12.8 %collective-permute-done.17.in2 = bf16[240,384]{1,0:T(8,128)(2,1)S(1)} collective-permute-done((bf16[240,384]{1,0:T(8,128)(2,1)S(1)}, bf16[240,384]{1,0:T(8,128)(2,1)S(1)}, u32[]{:S(2)}, u32[]{:S(2)}) %collective-permute-start.17) | collective-permute-done | bytes 184352 | tf_op jit(solution)/shard_map/ppermute | solution.py:32
  34.5 4.8 %assemble.1 = bf16[240,1920]{1,0:T(8,128)(2,1)S(1)} custom-call(s32[2,128]{1,0:T(2,128)S(1)} %make_plan.1.table, bf16[480,1920]{1,0:T(8,128)(2,1)S(1)} %bitcast.102, bf16[480,1920]{1,0:T(8,128)(2,1)} %collective-permute-done.12.other, bf16[240,384]{1,0:T(8,128)(2,1)S(1)} %collective-permute-done.16.in1, bf16[240,384]{1,0:T(8,128)(2,1)S(1)} %collective-permute-done.17.in2, ...), custom_call_target="tpu_custom_call" | custom-call | bytes 10485760 | tf_op jit(solution)/shard_map/assemble/pallas_call | solution.py:209
  39.4 2.1 %collective-permute-start.21 = (bf16[256,1920]{1,0:T(8,128)(2,1)S(1)}, bf16[256,1920]{1,0:T(8,128)(2,1)S(1)}, u32[]{:S(2)}, u32[]{:S(2)}) collective-permute-start(bf16[256,1920]{1,0:T(8,128)(2,1)S(1)} %pad_maximum_fusion), channel_id=1, source_target_pairs={{0,32},{32,64},{64,96},{96,0},{1,33},{33,65},{65,97},{97,1},{2,34}... | collective-permute-start | bytes 2949128 | tf_op jit(solution)/shard_map/ppermute | solution.py:32
  41.4 2.2 %collective-permute-start.22 = (bf16[256,1920]{1,0:T(8,128)(2,1)S(1)}, bf16[256,1920]{1,0:T(8,128)(2,1)}, u32[]{:S(2)}, u32[]{:S(2)}) collective-permute-start(bf16[256,1920]{1,0:T(8,128)(2,1)S(1)} %pad_maximum_fusion), channel_id=1, source_target_pairs={{0,96},{32,0},{64,32},{96,64},{1,97},{33,1},{65,33},{97,65},{2,98}... | collective-permute-start | bytes 2949128 | tf_op jit(solution)/shard_map/ppermute | solution.py:32
  44.3 1.6 collective-permute-start.19
  45.9 1.7 %collective-permute-start.20 = (bf16[240,1920]{1,0:T(8,128)(2,1)S(1)}, bf16[240,1920]{1,0:T(8,128)(2,1)S(1)}, u32[]{:S(2)}, u32[]{:S(2)}) collective-permute-start(bf16[240,1920]{1,0:T(8,128)(2,1)S(1)} %assemble.1), channel_id=1, source_target_pairs={{0,24},{8,0},{16,8},{24,16},{1,25},{9,1},{17,9},{25,17},{2,26},{10... | collective-permute-start | bytes 2764808 | tf_op jit(solution)/shard_map/ppermute | solution.py:32
  48.3 18.4 %collective-permute-done.19 = bf16[240,1920]{1,0:T(8,128)(2,1)S(1)} collective-permute-done((bf16[240,1920]{1,0:T(8,128)(2,1)S(1)}, bf16[240,1920]{1,0:T(8,128)(2,1)S(1)}, u32[]{:S(2)}, u32[]{:S(2)}) %collective-permute-start.19) | collective-permute-done | bytes 921632 | tf_op jit(solution)/shard_map/ppermute | solution.py:32
  66.8 1.6 collective-permute-start.23
  69.6 3.3 %collective-permute-start.26 = (bf16[128,1920]{1,0:T(8,128)(2,1)S(1)}, bf16[128,1920]{1,0:T(8,128)(2,1)S(1)}, u32[]{:S(2)}, u32[]{:S(2)}) collective-permute-start(bf16[128,1920]{1,0:T(8,128)(2,1)S(1)} %slice.70), channel_id=1, source_target_pairs={{0,96},{32,0},{64,32},{96,64},{1,97},{33,1},{65,33},{97,65},{2,98}... | collective-permute-start | bytes 1474568 | tf_op jit(solution)/shard_map/ppermute | solution.py:32
  72.9 1.7 %collective-permute-start.24 = (bf16[112,1920]{1,0:T(8,128)(2,1)S(1)}, bf16[112,1920]{1,0:T(8,128)(2,1)S(1)}, u32[]{:S(2)}, u32[]{:S(2)}) collective-permute-start(bf16[112,1920]{1,0:T(8,128)(2,1)S(1)} %slice.68), channel_id=1, source_target_pairs={{0,24},{8,0},{16,8},{24,16},{1,25},{9,1},{17,9},{25,17},{2,26},{10... | collective-permute-start | bytes 1290248 | tf_op jit(solution)/shard_map/ppermute | solution.py:32
  74.7 1.6 fusion.45
  76.2 5.2 %collective-permute-done.24 = bf16[112,1920]{1,0:T(8,128)(2,1)S(1)} collective-permute-done((bf16[112,1920]{1,0:T(8,128)(2,1)S(1)}, bf16[112,1920]{1,0:T(8,128)(2,1)S(1)}, u32[]{:S(2)}, u32[]{:S(2)}) %collective-permute-start.24) | collective-permute-done | bytes 430112 | tf_op jit(solution)/shard_map/ppermute | solution.py:32
  90.7 2.3 %collective-permute-start.32 = (s16[8,128,256]{2,1,0:T(8,128)(2,1)S(1)}, s16[8,128,256]{2,1,0:T(8,128)(2,1)S(1)}, u32[]{:S(2)}, u32[]{:S(2)}) collective-permute-start(s16[8,128,256]{2,1,0:T(8,128)(2,1)S(1)} %get-tuple-element.117), channel_id=1, source_target_pairs={{0,2},{2,4},{4,6},{6,0},{1,3},{3,5},{5,7},{7,1},{8,10},{10,12},{12... | collective-permute-start | bytes 1572872 | tf_op jit(solution)/shard_map/ppermute | solution.py:32
  93.1 2.5 %collective-permute-start.33 = (s16[8,128,256]{2,1,0:T(8,128)(2,1)S(1)}, s16[8,128,256]{2,1,0:T(8,128)(2,1)S(1)}, u32[]{:S(2)}, u32[]{:S(2)}) collective-permute-start(s16[8,128,256]{2,1,0:T(8,128)(2,1)S(1)} %get-tuple-element.118), channel_id=1, source_target_pairs={{0,6},{2,0},{4,2},{6,4},{1,7},{3,1},{5,3},{7,5},{8,14},{10,8},{12,... | collective-permute-start | bytes 1572872 | tf_op jit(solution)/shard_map/ppermute | solution.py:32
  96.5 7.9 %conditional.3 = (f32[256,240]{1,0:T(8,128)S(1)}, f32[256,240]{1,0:T(8,128)S(1)}, f32[256,240]{1,0:T(8,128)S(1)}, f32[256,240]{1,0:T(8,128)S(1)}, f32[256,240]{1...) conditional(s32[]{:T(128)} %bitcast.15, () %tuple.30, ...), branch_computations={%region_2.3_spmd, %region_3.4_spmd} | conditional | flops 3774873600 | bytes 34406528 | solution.py:433
  104.5 2.1 %fusion.77.refs_4_ = f32[256,240]{1,0:T(8,128)S(1)} fusion(bf16[256,1920]{1,0:T(8,128)(2,1)} %copy-done.4, bf16[240,1920]{1,0:T(8,128)(2,1)} %copy-done.7), kind=kOutput, calls=%fused_computation.133 | convolution fusion | flops 235929600 | bytes 2150400 | tf_op jit(solution)/shard_map/dot_general | solution.py:416
  107.6 3.1 %code_near.1 = (s16[8,256,256]{2,1,0:T(8,128)(2,1)S(1)}, s16[8,256,256]{2,1,0:T(8,128)(2,1)S(1)}) custom-call(f32[256,240]{1,0:T(8,128)S(1)} %get-tuple-element.143.refs_0_, f32[256,240]{1,0:T(8,128)S(1)} %get-tuple-element.144.refs_1_, f32[256,240]{1,0:T(8,128)S(1)} %get-tuple-element.145.refs_2_, f32[256,240]{1,0:T(8,128)S(1)} %get-tuple-element.146.refs_3_, ...), custom_call_target="tpu_custom_call" | custom-call | tf_op jit(solution)/shard_map/code_near/pallas_call | solution.py:314
  111.9 2.1 %collective-permute-start.35 = (s16[8,256,256]{2,1,0:T(8,128)(2,1)S(1)}, s16[8,256,256]{2,1,0:T(8,128)(2,1)S(1)}, u32[]{:S(2)}, u32[]{:S(2)}) collective-permute-start(s16[8,256,256]{2,1,0:T(8,128)(2,1)S(1)} %get-tuple-element.139), channel_id=1, source_target_pairs={{0,6},{2,0},{4,2},{6,4},{1,7},{3,1},{5,3},{7,5},{8,14},{10,8},{12,... | collective-permute-start | bytes 3145736 | tf_op jit(solution)/shard_map/ppermute | solution.py:32
  116.2 20.4 %collective-permute-done.34.refs_8_ = s16[8,256,256]{2,1,0:T(8,128)(2,1)S(1)} collective-permute-done((s16[8,256,256]{2,1,0:T(8,128)(2,1)S(1)}, s16[8,256,256]{2,1,0:T(8,128)(2,1)S(1)}, u32[]{:S(2)}, u32[]{:S(2)}) %collective-permute-start.34) | collective-permute-done | bytes 1048608 | tf_op jit(solution)/shard_map/ppermute | solution.py:32
  136.6 3.1 %code_last.1 = s16[16,8,16,256]{3,2,1,0:T(8,128)(2,1)} custom-call(f32[256,240]{1,0:T(8,128)S(1)} %fusion.73.refs_0_, f32[256,240]{1,0:T(8,128)S(1)} %fusion.74.refs_1_, f32[256,240]{1,0:T(8,128)S(1)} %fusion.75.refs_2_, f32[256,240]{1,0:T(8,128)S(1)} %fusion.76.refs_3_, f32[256,240]{1,0:T(8,128)S(1)} %fusion.77.refs_4_, f32[256,240]{1,0:T(8,128)S(1)} %fusion.78.refs_5_, ...), custom_call_target="tpu_custom_call" | custom-call | tf_op jit(solution)/shard_map/code_last/pallas_call | solution.py:328
  139.7 6.4 %all-to-all-start = ((s16[16,8,16,256]{3,2,1,0:T(8,128)(2,1)}), s16[16,8,16,256]{3,2,1,0:T(8,128)(2,1)S(1)}, u32[]{:S(2)}, u32[]{:S(2)}) async-start(s16[16,8,16,256]{3,2,1,0:T(8,128)(2,1)} %code_last.1), calls=%async_computation | async-start | bytes 2097152 | tf_op jit(solution)/shard_map/all_to_all | solution.py:437
  146.2 3.5 %reshape.104 = s32[16,8,16,4,2]{3,2,1,0,4:T(8,128)} reshape(s32[8192,2]{0,1:T(2,128)S(1)} %copy-done.16) | data formatting | bytes 131072 | tf_op jit(solution)/shard_map/reshape | solution.py:446
  155.8 6.6 %all-to-all-done.refs_0_ = s16[16,8,16,256]{3,2,1,0:T(8,128)(2,1)S(1)} async-done(((s16[16,8,16,256]{3,2,1,0:T(8,128)(2,1)}), s16[16,8,16,256]{3,2,1,0:T(8,128)(2,1)S(1)}, u32[]{:S(2)}, u32[]{:S(2)}) %all-to-all-start) | async-done | bytes 1048608 | tf_op jit(solution)/shard_map/all_to_all | solution.py:437
  162.4 5.5 %finish.1 = f32[64,7680]{1,0:T(8,128)} custom-call(s16[16,8,16,256]{3,2,1,0:T(8,128)(2,1)S(1)} %all-to-all-done.refs_0_, f32[1,7680]{1,0:T(1,128)S(1)} %add.109.refs_1_, f32[64,1]{1,0:T(8,128)S(1)} %broadcast_in_dim.55.refs_2_), custom_call_target="tpu_custom_call" | custom-call | tf_op jit(solution)/shard_map/finish/pallas_call | solution.py:357
  (142 shorter events, 35.7 us)
Async XLA Ops:
  0.0 151.0 %copy-start = (f32[200]{0:T(256)S(1)}, f32[200]{0:T(256)}, u32[]{:S(2)}) copy-start(f32[200]{0:T(256)} %param.16) | copy-start | bytes 2404
  0.0 4.1 %collective-permute-start.12 = (bf16[480,1920]{1,0:T(8,128)(2,1)}, bf16[480,1920]{1,0:T(8,128)(2,1)}, u32[]{:S(2)}, u32[]{:S(2)}) collective-permute-start(bf16[480,1920]{1,0:T(8,128)(2,1)} %bitcast.99), channel_id=1, source_target_pairs={{0,1},{1,0},{2,3},{3,2},{4,5},{5,4},{6,7},{7,6},{8,9},{9,8},{10,11... | collective-permute-start | bytes 5529608 | tf_op jit(solution)/shard_map/ppermute | solution.py:36
  5.7 28.7 %copy-start.2 = (bf16[1,480,1920]{2,1,0:T(8,128)(2,1)S(1)}, bf16[1,480,1920]{2,1,0:T(8,128)(2,1)}, u32[]{:S(2)}) copy-start(bf16[1,480,1920]{2,1,0:T(8,128)(2,1)} %param.12) | copy-start | bytes 5529604
  9.7 8.9 %collective-permute-start.16 = (bf16[240,384]{1,0:T(8,128)(2,1)S(1)}, bf16[240,384]{1,0:T(8,128)(2,1)S(1)}, u32[]{:S(2)}, u32[]{:S(2)}) collective-permute-start(bf16[240,384]{1,0:T(8,128)(2,1)S(1)} %get-tuple-element.101.after), channel_id=1, source_target_pairs={{0,2},{2,4},{4,6},{6,0},{1,3},{3,5},{5,7},{7,1},{8,10},{10,12},{12... | collective-permute-start | bytes 552968 | tf_op jit(solution)/shard_map/ppermute | solution.py:32
  12.9 26.4 %collective-permute-start.13 = (bf16[64,1920]{1,0:T(8,128)(2,1)S(1)}, bf16[64,1920]{1,0:T(8,128)(2,1)S(1)}, u32[]{:S(2)}, u32[]{:S(2)}) collective-permute-start(bf16[64,1920]{1,0:T(8,128)(2,1)S(1)} %get-tuple-element.102), channel_id=1, source_target_pairs={{0,4},{2,6},{4,0},{6,2},{1,5},{3,7},{5,1},{7,3},{8,12},{10,14},{12... | collective-permute-start | bytes 737288 | tf_op jit(solution)/shard_map/ppermute | solution.py:32
  15.7 23.6 %collective-permute-start.14 = (bf16[64,1920]{1,0:T(8,128)(2,1)S(1)}, bf16[64,1920]{1,0:T(8,128)(2,1)S(1)}, u32[]{:S(2)}, u32[]{:S(2)}) collective-permute-start(bf16[64,1920]{1,0:T(8,128)(2,1)S(1)} %get-tuple-element.103), channel_id=1, source_target_pairs={{0,6},{2,0},{4,2},{6,4},{1,7},{3,1},{5,3},{7,5},{8,14},{10,8},{12,... | collective-permute-start | bytes 737288 | tf_op jit(solution)/shard_map/ppermute | solution.py:32
  17.2 22.1 %collective-permute-start.15 = (bf16[64,1920]{1,0:T(8,128)(2,1)S(1)}, bf16[64,1920]{1,0:T(8,128)(2,1)S(1)}, u32[]{:S(2)}, u32[]{:S(2)}) collective-permute-start(bf16[64,1920]{1,0:T(8,128)(2,1)S(1)} %get-tuple-element.104), channel_id=1, source_target_pairs={{0,2},{2,4},{4,6},{6,0},{1,3},{3,5},{5,7},{7,1},{8,10},{10,12},{12... | collective-permute-start | bytes 737288 | tf_op jit(solution)/shard_map/ppermute | solution.py:32
  17.7 15.5 %collective-permute-start.17 = (bf16[240,384]{1,0:T(8,128)(2,1)S(1)}, bf16[240,384]{1,0:T(8,128)(2,1)S(1)}, u32[]{:S(2)}, u32[]{:S(2)}) collective-permute-start(bf16[240,384]{1,0:T(8,128)(2,1)S(1)} %get-tuple-element.106), channel_id=1, source_target_pairs={{0,4},{2,6},{4,0},{6,2},{1,5},{3,7},{5,1},{7,3},{8,12},{10,14},{12... | collective-permute-start | bytes 552968 | tf_op jit(solution)/shard_map/ppermute | solution.py:32
  18.6 15.8 %collective-permute-start.18 = (bf16[240,384]{1,0:T(8,128)(2,1)S(1)}, bf16[240,384]{1,0:T(8,128)(2,1)S(1)}, u32[]{:S(2)}, u32[]{:S(2)}) collective-permute-start(bf16[240,384]{1,0:T(8,128)(2,1)S(1)} %get-tuple-element.107), channel_id=1, source_target_pairs={{0,6},{2,0},{4,2},{6,4},{1,7},{3,1},{5,3},{7,5},{8,14},{10,8},{12,... | collective-permute-start | bytes 552968 | tf_op jit(solution)/shard_map/ppermute | solution.py:32
  39.4 27.4 %collective-permute-start.21 = (bf16[256,1920]{1,0:T(8,128)(2,1)S(1)}, bf16[256,1920]{1,0:T(8,128)(2,1)S(1)}, u32[]{:S(2)}, u32[]{:S(2)}) collective-permute-start(bf16[256,1920]{1,0:T(8,128)(2,1)S(1)} %pad_maximum_fusion), channel_id=1, source_target_pairs={{0,32},{32,64},{64,96},{96,0},{1,33},{33,65},{65,97},{97,1},{2,34}... | collective-permute-start | bytes 2949128 | tf_op jit(solution)/shard_map/ppermute | solution.py:32
  41.4 25.3 %collective-permute-start.22 = (bf16[256,1920]{1,0:T(8,128)(2,1)S(1)}, bf16[256,1920]{1,0:T(8,128)(2,1)}, u32[]{:S(2)}, u32[]{:S(2)}) collective-permute-start(bf16[256,1920]{1,0:T(8,128)(2,1)S(1)} %pad_maximum_fusion), channel_id=1, source_target_pairs={{0,96},{32,0},{64,32},{96,64},{1,97},{33,1},{65,33},{97,65},{2,98}... | collective-permute-start | bytes 2949128 | tf_op jit(solution)/shard_map/ppermute | solution.py:32
  44.3 22.4 %collective-permute-start.19 = (bf16[240,1920]{1,0:T(8,128)(2,1)S(1)}, bf16[240,1920]{1,0:T(8,128)(2,1)S(1)}, u32[]{:S(2)}, u32[]{:S(2)}) collective-permute-start(bf16[240,1920]{1,0:T(8,128)(2,1)S(1)} %assemble.1), channel_id=1, source_target_pairs={{0,8},{8,16},{16,24},{24,0},{1,9},{9,17},{17,25},{25,1},{2,10},{10... | collective-permute-start | bytes 2764808 | tf_op jit(solution)/shard_map/ppermute | solution.py:32
  45.9 20.8 %collective-permute-start.20 = (bf16[240,1920]{1,0:T(8,128)(2,1)S(1)}, bf16[240,1920]{1,0:T(8,128)(2,1)S(1)}, u32[]{:S(2)}, u32[]{:S(2)}) collective-permute-start(bf16[240,1920]{1,0:T(8,128)(2,1)S(1)} %assemble.1), channel_id=1, source_target_pairs={{0,24},{8,0},{16,8},{24,16},{1,25},{9,1},{17,9},{25,17},{2,26},{10... | collective-permute-start | bytes 2764808 | tf_op jit(solution)/shard_map/ppermute | solution.py:32
  48.2 37.9 %collective-permute-start.27 = (bf16[240,1920]{1,0:T(8,128)(2,1)S(1)}, bf16[240,1920]{1,0:T(8,128)(2,1)S(1)}, u32[]{:S(2)}, u32[]{:S(2)}) collective-permute-start(bf16[240,1920]{1,0:T(8,128)(2,1)S(1)} %assemble.1), channel_id=1, source_target_pairs={{0,1},{1,0},{2,3},{3,2},{4,5},{5,4},{6,7},{7,6},{8,9},{9,8},{10,11... | collective-permute-start | bytes 2764808 | tf_op jit(solution)/shard_map/ppermute | solution.py:36
  66.7 29.8 %copy-start.8 = (bf16[240,1920]{1,0:T(8,128)(2,1)}, bf16[240,1920]{1,0:T(8,128)(2,1)S(1)}, u32[]{:S(2)}) copy-start(bf16[240,1920]{1,0:T(8,128)(2,1)S(1)} %collective-permute-done.20) | copy-start | bytes 2764804
  66.8 14.7 %collective-permute-start.23 = (bf16[128,1920]{1,0:T(8,128)(2,1)S(1)}, bf16[128,1920]{1,0:T(8,128)(2,1)S(1)}, u32[]{:S(2)}, u32[]{:S(2)}) collective-permute-start(bf16[128,1920]{1,0:T(8,128)(2,1)S(1)} %slice.67), channel_id=1, source_target_pairs={{0,8},{8,16},{16,24},{24,0},{1,9},{9,17},{17,25},{25,1},{2,10},{10... | collective-permute-start | bytes 1474568 | tf_op jit(solution)/shard_map/ppermute | solution.py:32
  68.5 13.5 %collective-permute-start.25 = (bf16[128,1920]{1,0:T(8,128)(2,1)S(1)}, bf16[128,1920]{1,0:T(8,128)(2,1)S(1)}, u32[]{:S(2)}, u32[]{:S(2)}) collective-permute-start(bf16[128,1920]{1,0:T(8,128)(2,1)S(1)} %slice.69), channel_id=1, source_target_pairs={{0,32},{32,64},{64,96},{96,0},{1,33},{33,65},{65,97},{97,1},{2,34}... | collective-permute-start | bytes 1474568 | tf_op jit(solution)/shard_map/ppermute | solution.py:32
  69.6 12.4 %collective-permute-start.26 = (bf16[128,1920]{1,0:T(8,128)(2,1)S(1)}, bf16[128,1920]{1,0:T(8,128)(2,1)S(1)}, u32[]{:S(2)}, u32[]{:S(2)}) collective-permute-start(bf16[128,1920]{1,0:T(8,128)(2,1)S(1)} %slice.70), channel_id=1, source_target_pairs={{0,96},{32,0},{64,32},{96,64},{1,97},{33,1},{65,33},{97,65},{2,98}... | collective-permute-start | bytes 1474568 | tf_op jit(solution)/shard_map/ppermute | solution.py:32
  72.9 8.5 %collective-permute-start.24 = (bf16[112,1920]{1,0:T(8,128)(2,1)S(1)}, bf16[112,1920]{1,0:T(8,128)(2,1)S(1)}, u32[]{:S(2)}, u32[]{:S(2)}) collective-permute-start(bf16[112,1920]{1,0:T(8,128)(2,1)S(1)} %slice.68), channel_id=1, source_target_pairs={{0,24},{8,0},{16,8},{24,16},{1,25},{9,1},{17,9},{25,17},{2,26},{10... | collective-permute-start | bytes 1290248 | tf_op jit(solution)/shard_map/ppermute | solution.py:32
  81.5 6.6 %collective-permute-start.31 = (bf16[240,1920]{1,0:T(8,128)(2,1)S(1)}, bf16[240,1920]{1,0:T(8,128)(2,1)S(1)}, u32[]{:S(2)}, u32[]{:S(2)}) collective-permute-start(bf16[240,1920]{1,0:T(8,128)(2,1)S(1)} %collective-permute-done.19), channel_id=1, source_target_pairs={{0,1},{1,0},{2,3},{3,2},{4,5},{5,4},{6,7},{7,6},{8,9},{9,8},{10,11... | collective-permute-start | bytes 2764808 | tf_op jit(solution)/shard_map/ppermute | solution.py:36
  81.5 7.1 %collective-permute-start.28 = (bf16[240,1920]{1,0:T(8,128)(2,1)S(1)}, bf16[240,1920]{1,0:T(8,128)(2,1)S(1)}, u32[]{:S(2)}, u32[]{:S(2)}) collective-permute-start(bf16[240,1920]{1,0:T(8,128)(2,1)S(1)} %collective-permute-done.20), channel_id=1, source_target_pairs={{0,1},{1,0},{2,3},{3,2},{4,5},{5,4},{6,7},{7,6},{8,9},{9,8},{10,11... | collective-permute-start | bytes 2764808 | tf_op jit(solution)/shard_map/ppermute | solution.py:36
  82.0 7.1 %collective-permute-start.29 = (bf16[128,1920]{1,0:T(8,128)(2,1)S(1)}, bf16[128,1920]{1,0:T(8,128)(2,1)S(1)}, u32[]{:S(2)}, u32[]{:S(2)}) collective-permute-start(bf16[128,1920]{1,0:T(8,128)(2,1)S(1)} %collective-permute-done.23), channel_id=1, source_target_pairs={{0,1},{1,0},{2,3},{3,2},{4,5},{5,4},{6,7},{7,6},{8,9},{9,8},{10,11... | collective-permute-start | bytes 1474568 | tf_op jit(solution)/shard_map/ppermute | solution.py:36
  83.9 5.2 %collective-permute-start.30 = (bf16[112,1920]{1,0:T(8,128)(2,1)S(1)}, bf16[112,1920]{1,0:T(8,128)(2,1)S(1)}, u32[]{:S(2)}, u32[]{:S(2)}) collective-permute-start(bf16[112,1920]{1,0:T(8,128)(2,1)S(1)} %collective-permute-done.24), channel_id=1, source_target_pairs={{0,1},{1,0},{2,3},{3,2},{4,5},{5,4},{6,7},{7,6},{8,9},{9,8},{10,11... | collective-permute-start | bytes 1290248 | tf_op jit(solution)/shard_map/ppermute | solution.py:36
  84.4 12.1 %copy-start.7 = (bf16[240,1920]{1,0:T(8,128)(2,1)}, bf16[240,1920]{1,0:T(8,128)(2,1)S(1)}, u32[]{:S(2)}) copy-start(bf16[240,1920]{1,0:T(8,128)(2,1)S(1)} %constant_dynamic-update-slice_fusion) | copy-start | bytes 2764804
  85.6 10.4 %copy-start.4 = (bf16[256,1920]{1,0:T(8,128)(2,1)}, bf16[256,1920]{1,0:T(8,128)(2,1)S(1)}, u32[]{:S(2)}) copy-start(bf16[256,1920]{1,0:T(8,128)(2,1)S(1)} %convolution_convert_fusion.1) | copy-start | bytes 2949124
  86.1 10.4 %copy-start.10 = (bf16[240,1920]{1,0:T(8,128)(2,1)}, bf16[240,1920]{1,0:T(8,128)(2,1)S(1)}, u32[]{:S(2)}) copy-start(bf16[240,1920]{1,0:T(8,128)(2,1)S(1)} %collective-permute-done.27) | copy-start | bytes 2764804
  88.1 8.4 %copy-start.12 = (bf16[240,1920]{1,0:T(8,128)(2,1)}, bf16[240,1920]{1,0:T(8,128)(2,1)S(1)}, u32[]{:S(2)}) copy-start(bf16[240,1920]{1,0:T(8,128)(2,1)S(1)} %collective-permute-done.31) | copy-start | bytes 2764804
  90.7 16.9 %collective-permute-start.32 = (s16[8,128,256]{2,1,0:T(8,128)(2,1)S(1)}, s16[8,128,256]{2,1,0:T(8,128)(2,1)S(1)}, u32[]{:S(2)}, u32[]{:S(2)}) collective-permute-start(s16[8,128,256]{2,1,0:T(8,128)(2,1)S(1)} %get-tuple-element.117), channel_id=1, source_target_pairs={{0,2},{2,4},{4,6},{6,0},{1,3},{3,5},{5,7},{7,1},{8,10},{10,12},{12... | collective-permute-start | bytes 1572872 | tf_op jit(solution)/shard_map/ppermute | solution.py:32
  93.1 14.6 %collective-permute-start.33 = (s16[8,128,256]{2,1,0:T(8,128)(2,1)S(1)}, s16[8,128,256]{2,1,0:T(8,128)(2,1)S(1)}, u32[]{:S(2)}, u32[]{:S(2)}) collective-permute-start(s16[8,128,256]{2,1,0:T(8,128)(2,1)S(1)} %get-tuple-element.118), channel_id=1, source_target_pairs={{0,6},{2,0},{4,2},{6,4},{1,7},{3,1},{5,3},{7,5},{8,14},{10,8},{12,... | collective-permute-start | bytes 1572872 | tf_op jit(solution)/shard_map/ppermute | solution.py:32
  110.7 25.9 %collective-permute-start.34 = (s16[8,256,256]{2,1,0:T(8,128)(2,1)S(1)}, s16[8,256,256]{2,1,0:T(8,128)(2,1)S(1)}, u32[]{:S(2)}, u32[]{:S(2)}) collective-permute-start(s16[8,256,256]{2,1,0:T(8,128)(2,1)S(1)} %get-tuple-element.138), channel_id=1, source_target_pairs={{0,2},{2,4},{4,6},{6,0},{1,3},{3,5},{5,7},{7,1},{8,10},{10,12},{12... | collective-permute-start | bytes 3145736 | tf_op jit(solution)/shard_map/ppermute | solution.py:32
  111.9 24.7 %collective-permute-start.35 = (s16[8,256,256]{2,1,0:T(8,128)(2,1)S(1)}, s16[8,256,256]{2,1,0:T(8,128)(2,1)S(1)}, u32[]{:S(2)}, u32[]{:S(2)}) collective-permute-start(s16[8,256,256]{2,1,0:T(8,128)(2,1)S(1)} %get-tuple-element.139), channel_id=1, source_target_pairs={{0,6},{2,0},{4,2},{6,4},{1,7},{3,1},{5,3},{7,5},{8,14},{10,8},{12,... | collective-permute-start | bytes 3145736 | tf_op jit(solution)/shard_map/ppermute | solution.py:32
  139.7 22.7 %all-to-all-start = ((s16[16,8,16,256]{3,2,1,0:T(8,128)(2,1)}), s16[16,8,16,256]{3,2,1,0:T(8,128)(2,1)S(1)}, u32[]{:S(2)}, u32[]{:S(2)}) async-start(s16[16,8,16,256]{3,2,1,0:T(8,128)(2,1)} %code_last.1), calls=%async_computation | async-start | bytes 2097152 | tf_op jit(solution)/shard_map/all_to_all | solution.py:437
  (12 other events, 52.6 us)
